TPU v7x, 256 devices: a whole 4x4x8 slice. The times are simulated.
256 devices in a mesh: blk: 16 (over y_hi, z), frames: 16 (over x, y_lo, core).
Axes of the slice: x: 4, y: 4 (y_hi: 2, y_lo: 2; y = y_hi * 2 + y_lo), z: 8, core: 2. Of those that a mesh axis runs over, the one named last changes fastest.
Arguments:
- coarse_query: bfloat16 [512, 16, 256], P('blk'), may hold values from -125 to 125
- coarse_feat: bfloat16 [64, 8160, 256], P('frames', 'blk'), may hold values from -61 to 61
- fine_query: bfloat16 [512, 128], P(('blk', 'frames')), may hold values from -175 to 175
- fine_tiles: bfloat16 [64, 1024, 64, 128], P('frames', 'blk'), may hold values from -61 to 61
- track_pos: int32 [2, 64, 512], P(None, None, ('blk', 'frames')), may hold values from 0 to 959, as said below
- tile_list: int32 [64, 16, 16, 8], P('frames', 'blk'), may hold values from 0 to 63, as said below
- tile_valid: int32 [64, 16, 16, 8], P('frames', 'blk'), may hold values from 0 to 1, as said below
Outputs:
- coarse_pos: float32 [2, 64, 512], P(None, 'frames', 'blk')
- fine_offset: float32 [2, 64, 512], P(None, None, ('blk', 'frames'))
Inputs may be any that keep to these rules, and one draw needn't show every extreme that they name: `tile_list`: in each list the valid slots come first and name distinct tiles of the group's window; padded slots hold 63; in every frame and group some owner's list is full. `tile_valid`: each list has at least 4 valid slots. `track_pos`: rows lie below 544 and columns below 960.
All inputs are finite; a program needn't handle non-finite values.
Results may differ from a plain program's by a relative error of at most 0.0003.
Values may be sent and summed in bfloat16 or wider, within the bound.
A program may use at most 192 MiB of HBM per device.

v0:
```python
import math
import jax
import jax.numpy as jnp
from jax import lax
from jax.sharding import PartitionSpec as P

GH = 68
GW = 120
TILE = 8
spread_cells = 32.0


def refine_frame(descriptors, tile_block, tile_ids, tile_live, track_row, track_col, base_cell):
    slot_count, cell_count, channels = tile_block.shape
    flat_tiles = tile_block.reshape(slot_count * cell_count, channels)
    scores = jnp.einsum(
        "nc,kc->nk", descriptors, flat_tiles, preferred_element_type=jnp.float32
    ) * (1.0 / math.sqrt(channels))
    global_cell = base_cell + tile_ids
    inner_cell = jnp.arange(cell_count, dtype=jnp.int32)
    cell_row = (global_cell // GW * TILE)[:, None] + (inner_cell // TILE)[None, :]
    cell_col = (global_cell % GW * TILE)[:, None] + (inner_cell % TILE)[None, :]
    cell_row = cell_row.reshape(-1).astype(jnp.float32)
    cell_col = cell_col.reshape(-1).astype(jnp.float32)
    distance = (cell_row[None, :] - track_row[:, None]) ** 2 + (
        cell_col[None, :] - track_col[:, None]
    ) ** 2
    scores = scores - distance * (0.5 / (spread_cells * spread_cells))
    live_cells = jnp.broadcast_to(tile_live[:, None] > 0, (slot_count, cell_count)).reshape(-1)
    scores = jnp.where(live_cells[None, :], scores, -1e30)
    highest = jnp.max(scores, axis=1, keepdims=True)
    weights = jnp.exp(scores - highest)
    totals = jnp.sum(weights, axis=1)
    mean_row = jnp.sum(weights * cell_row[None, :], axis=1) / totals
    mean_col = jnp.sum(weights * cell_col[None, :], axis=1) / totals
    return ((mean_row - track_row) / spread_cells, (mean_col - track_col) / spread_cells)


def coarse_finish(row_mean, col_mean):
    row_heads = jnp.mean(row_mean, axis=2)
    col_heads = jnp.mean(col_mean, axis=2)
    return jnp.stack(
        [(row_heads - (GH - 1) / 2.0) / (GH / 4.0), (col_heads - (GW - 1) / 2.0) / (GW / 4.0)]
    )


def body(coarse_query, coarse_feat, fine_query, fine_tiles, track_pos, tile_list, tile_valid):
    track_group, heads, channels = coarse_query.shape
    frames_here, region, _ = coarse_feat.shape
    scale = 1.0 / math.sqrt(channels)
    group_start = lax.axis_index("blk") * region
    query_rows = coarse_query.reshape(track_group * heads, channels)
    row_count = query_rows.shape[0]
    zeros_state = jnp.zeros((frames_here, row_count), jnp.float32)
    shard_piece = lax.all_gather(coarse_feat, "blk", axis=1, tiled=True)
    first_pos = jnp.int32(0)
    maxima = jnp.full((frames_here, row_count), -jnp.inf, jnp.float32)
    totals = zeros_state
    row_sums = zeros_state
    col_sums = zeros_state
    length = shard_piece.shape[1]
    for offset in range(0, length, 512):
        feat_block = shard_piece[:, offset : offset + 512]
        scores = (
            jnp.einsum("rc,fpc->frp", query_rows, feat_block, preferred_element_type=jnp.float32)
            * scale
        )
        positions = first_pos + offset + jnp.arange(feat_block.shape[1], dtype=jnp.int32)
        pos_row = (positions // GW).astype(jnp.float32)
        pos_col = (positions % GW).astype(jnp.float32)
        new_max = jnp.maximum(maxima, jnp.max(scores, axis=2))
        retain = jnp.exp(maxima - new_max)
        weights = jnp.exp(scores - new_max[:, :, None])
        totals = totals * retain + jnp.sum(weights, axis=2)
        row_sums = row_sums * retain + jnp.sum(weights * pos_row[None, None, :], axis=2)
        col_sums = col_sums * retain + jnp.sum(weights * pos_col[None, None, :], axis=2)
        maxima = new_max
    final_state = (maxima, totals, row_sums, col_sums)
    row_mean = (final_state[2] / final_state[1]).reshape(frames_here, track_group, heads)
    col_mean = (final_state[3] / final_state[1]).reshape(frames_here, track_group, heads)
    coarse_pos = coarse_finish(row_mean, col_mean)
    list_ids = jnp.transpose(tile_list[:, 0], (1, 0, 2))
    list_live = jnp.transpose(tile_valid[:, 0], (1, 0, 2))
    picked = fine_tiles[jnp.arange(frames_here, dtype=jnp.int32)[None, :, None], list_ids]
    per_frame = jax.vmap(refine_frame, in_axes=(None, 0, 0, 0, 0, 0, None))
    got_tiles, got_ids, got_live = (
        lax.all_to_all(picked, "frames", split_axis=0, concat_axis=0, tiled=True),
        lax.all_to_all(list_ids, "frames", split_axis=0, concat_axis=0, tiled=True),
        lax.all_to_all(list_live, "frames", split_axis=0, concat_axis=0, tiled=True),
    )
    window = got_tiles.shape[0] * got_tiles.shape[1]
    got_tiles = got_tiles.reshape((window,) + got_tiles.shape[2:])
    got_ids = got_ids.reshape(window, -1)
    got_live = got_live.reshape(window, -1)
    places = track_pos.astype(jnp.float32)
    rows_out, cols_out = per_frame(
        fine_query, got_tiles, got_ids, got_live, places[0], places[1], group_start
    )
    fine_offset = jnp.stack([rows_out, cols_out])
    return (coarse_pos, fine_offset)


def solution(mesh):
    return jax.shard_map(
        body,
        mesh=mesh,
        in_specs=(
            P("blk", None, None),
            P("frames", "blk", None),
            P(("blk", "frames"), None),
            P("frames", "blk", None, None),
            P(None, None, ("blk", "frames")),
            P("frames", "blk", None, None),
            P("frames", "blk", None, None),
        ),
        out_specs=(P(None, "frames", "blk"), P(None, None, ("blk", "frames"))),
        check_vma=False,
    )
```

profile of v0, /device:TPU:1, one launch (start us, length us, event | category | flops | bytes accessed | tf_op | source)
XLA Modules:
  0.0 419.7 jit_solution(9521634388056625112)
XLA Ops:
  9.3 6.8 %all-to-all-start.2 = ((s32[16,4,8]{2,1,0:T(4,128)}), s32[16,4,8]{2,1,0:T(4,128)S(1)}, u32[]{:S(2)}, u32[]{:S(2)}) async-start(s32[16,4,8]{2,1,0:T(4,128)} %bitcast.25), calls=%async_computation.2 | async-start | bytes 65536 | tf_op jit(solution)/shard_map/all_to_all | solution.py:88
  17.5 4.4 %all-to-all-done.2 = s32[16,4,8]{2,1,0:T(4,128)S(1)} async-done(((s32[16,4,8]{2,1,0:T(4,128)}), s32[16,4,8]{2,1,0:T(4,128)S(1)}, u32[]{:S(2)}, u32[]{:S(2)}) %all-to-all-start.2) | async-done | bytes 2080 | tf_op jit(solution)/shard_map/all_to_all | solution.py:88
  22.0 3.7 all-to-all-start
  26.5 10.3 %gather_fusion = bf16[512,64,128]{2,1,0:T(8,128)(2,1)} fusion(bf16[4,64,64,128]{3,2,1,0:T(8,128)(2,1)} %param.10, s32[512]{0:T(512)S(1)} %reshape.890), kind=kCustom, calls=%fused_computation | custom fusion | bytes 16781312 | tf_op jit(solution)/shard_map/gather | solution.py:84
  36.8 5.9 %all-to-all-start.1 = ((bf16[16,4,8,64,128]{4,3,2,1,0:T(8,128)(2,1)}), bf16[16,4,8,64,128]{4,3,2,1,0:T(8,128)(2,1)}, u32[]{:S(2)}, u32[]{:S(2)}) async-start(bf16[16,4,8,64,128]{4,3,2,1,0:T(8,128)(2,1)} %bitcast.260), calls=%async_computation.1 | async-start | bytes 16777216 | tf_op jit(solution)/shard_map/all_to_all | solution.py:87
  44.4 129.9 %all-to-all-done.1 = bf16[16,4,8,64,128]{4,3,2,1,0:T(8,128)(2,1)} async-done(((bf16[16,4,8,64,128]{4,3,2,1,0:T(8,128)(2,1)}), bf16[16,4,8,64,128]{4,3,2,1,0:T(8,128)(2,1)}, u32[]{:S(2)}, u32[]{:S(2)}) %all-to-all-start.1) | async-done | bytes 8388640 | tf_op jit(solution)/shard_map/all_to_all | solution.py:87
  174.3 5.8 %multiply_reduce_fusion.33 = (f32[64,2]{1,0:T(8,128)S(1)}, f32[64,2]{1,0:T(8,128)S(1)}, f32[64,2]{1,0:T(8,128)S(1)}) fusion(f32[64,512]{1,0:T(8,128)S(1)} %get-tuple-element.151, f32[64,512]{1,0:T(8,128)S(1)} %get-tuple-element.150, bf16[64,512,128]{2,1,0:T(8,128)(2,1)} %bitcast.29, pred[64,512]{1,0:T(8,128)(4,1)S(1)} %broadcast_in_dim.23, ...), kind=kOutput, calls=%fused_computation.137 | convolution fusion | flops 17760512 | bytes 8686592 | tf_op jit(solution)/shard_map/vmap()/sub | solution.py:32
  180.9 113.8 %all-gather.2.cloned.1.call-done = bf16[4,8160,256]{2,0,1:T(4,128)(2,1)} async-done(((bf16[4,510,256]{2,0,1:T(4,128)(2,1)}), bf16[4,8160,256]{2,0,1:T(4,128)(2,1)}) %all-gather.2.cloned.1.call-update) | async-done | bytes 16711696 | tf_op jit(solution)/shard_map/all_gather | solution.py:55
  298.8 10.4 %fusion.197 = (bf16[4,512,256]{2,0,1:T(4,128)(2,1)S(1)}, bf16[4,512,256]{2,0,1:T(4,128)(2,1)S(1)}, bf16[4,512,256]{2,0,1:T(4,128)(2,1)S(1)}, bf16[4,512,256]{2,0...) fusion(bf16[4,8160,256]{2,0,1:T(4,128)(2,1)} %all-gather.2.clon, ...), kind=kLoop, calls=%fused_computation.377 | loop fusion | bytes 31457280 | tf_op jit(solution)/shard_map/slice | solution.py:63
  309.2 2.7 bitcast_reduce_fusion
  311.9 2.7 bitcast_reduce_fusion.1
  320.0 2.7 bitcast_reduce_fusion.4
  322.8 2.7 bitcast_reduce_fusion.5
  328.2 2.8 bitcast_reduce_fusion.7
  339.0 2.8 bitcast_reduce_fusion.11
  351.4 3.8 multiply_reduce_fusion.31
  355.3 6.8 %multiply_reduce_fusion.15 = (f32[4,512]{1,0:T(4,128)S(1)}, f32[4,512]{1,0:T(4,128)S(1)}, f32[4,512]{1,0:T(4,128)S(1)}, f32[4,512]{1,0:T(4,128)S(1)}, f32[4,512]{1,0:T(4,128)S(1)}, /*index=5*/f32[4,512]{1,0:T(4,128)S(1)}) fusion(f32[4,512,512]{2,1,0:T(8,128)} %get-tuple-element.96, f32[512]{0:T(512)S(1)} %fusion.108, f32[4,512]{1,0:T(4,128)S(1)} %get-tuple-element.54, ...), kind=kLoop, calls=%fused_computation.62 | loop fusion | flops 14667776 | bytes 8462336 | tf_op jit(solution)/shard_map/reduce_sum | solution.py:75
  362.3 6.8 %multiply_reduce_fusion.17 = (f32[4,512]{1,0:T(4,128)S(1)}, f32[4,512]{1,0:T(4,128)S(1)}, f32[4,512]{1,0:T(4,128)S(1)}, f32[4,512]{1,0:T(4,128)S(1)}, f32[4,512]{1,0:T(4,128)S(1)}, /*index=5*/f32[4,512]{1,0:T(4,128)S(1)}) fusion(f32[4,512,512]{2,1,0:T(8,128)} %get-tuple-element.100, f32[512]{0:T(512)S(1)} %fusion.116, f32[4,512]{1,0:T(4,128)S(1)} %get-tuple-element.56, ...), kind=kLoop, calls=%fused_computation.64 | loop fusion | flops 14667776 | bytes 8462336 | tf_op jit(solution)/shard_map/reduce_sum | solution.py:75
  369.2 6.8 %multiply_reduce_fusion.19 = (f32[4,512]{1,0:T(4,128)S(1)}, f32[4,512]{1,0:T(4,128)S(1)}, f32[4,512]{1,0:T(4,128)S(1)}, f32[4,512]{1,0:T(4,128)S(1)}, f32[4,512]{1,0:T(4,128)S(1)}, /*index=5*/f32[4,512]{1,0:T(4,128)S(1)}) fusion(f32[4,512,512]{2,1,0:T(8,128)} %get-tuple-element.104, f32[512]{0:T(512)S(1)} %fusion.124, f32[4,512]{1,0:T(4,128)S(1)} %get-tuple-element.58, ...), kind=kLoop, calls=%fused_computation.66 | loop fusion | flops 14667776 | bytes 8462336 | tf_op jit(solution)/shard_map/reduce_sum | solution.py:75
  376.2 6.8 %multiply_reduce_fusion.21 = (f32[4,512]{1,0:T(4,128)S(1)}, f32[4,512]{1,0:T(4,128)S(1)}, f32[4,512]{1,0:T(4,128)S(1)}, f32[4,512]{1,0:T(4,128)S(1)}, f32[4,512]{1,0:T(4,128)S(1)}, /*index=5*/f32[4,512]{1,0:T(4,128)S(1)}) fusion(f32[4,512,512]{2,1,0:T(8,128)} %get-tuple-element.108, f32[512]{0:T(512)S(1)} %fusion.132, f32[4,512]{1,0:T(4,128)S(1)} %get-tuple-element.60, ...), kind=kLoop, calls=%fused_computation.68 | loop fusion | flops 14667776 | bytes 8462336 | tf_op jit(solution)/shard_map/reduce_sum | solution.py:75
  383.2 7.0 %multiply_reduce_fusion.23 = (f32[4,512]{1,0:T(4,128)S(1)}, f32[4,512]{1,0:T(4,128)S(1)}, f32[4,512]{1,0:T(4,128)S(1)}, f32[4,512]{1,0:T(4,128)S(1)}, f32[4,512]{1,0:T(4,128)S(1)}, /*index=5*/f32[4,512]{1,0:T(4,128)S(1)}) fusion(f32[4,512,512]{2,1,0:T(8,128)} %get-tuple-element.112, f32[512]{0:T(512)S(1)} %fusion.140, f32[4,512]{1,0:T(4,128)S(1)} %get-tuple-element.62, ...), kind=kLoop, calls=%fused_computation.70 | loop fusion | flops 14667776 | bytes 8462336 | tf_op jit(solution)/shard_map/reduce_sum | solution.py:75
  390.3 6.8 %multiply_reduce_fusion.25 = (f32[4,512]{1,0:T(4,128)S(1)}, f32[4,512]{1,0:T(4,128)S(1)}, f32[4,512]{1,0:T(4,128)S(1)}, f32[4,512]{1,0:T(4,128)S(1)}, f32[4,512]{1,0:T(4,128)S(1)}, /*index=5*/f32[4,512]{1,0:T(4,128)S(1)}) fusion(f32[4,512,512]{2,1,0:T(8,128)} %get-tuple-element.116, f32[512]{0:T(512)S(1)} %fusion.148, f32[4,512]{1,0:T(4,128)S(1)} %get-tuple-element.64, ...), kind=kLoop, calls=%fused_computation.72 | loop fusion | flops 14667776 | bytes 8462336 | tf_op jit(solution)/shard_map/reduce_sum | solution.py:75
  397.3 6.8 %multiply_reduce_fusion.27 = (f32[4,512]{1,0:T(4,128)S(1)}, f32[4,512]{1,0:T(4,128)S(1)}, f32[4,512]{1,0:T(4,128)S(1)}, f32[4,512]{1,0:T(4,128)S(1)}, f32[4,512]{1,0:T(4,128)S(1)}, /*index=5*/f32[4,512]{1,0:T(4,128)S(1)}) fusion(f32[4,512,512]{2,1,0:T(8,128)} %get-tuple-element.120, f32[512]{0:T(512)S(1)} %fusion.156, f32[4,512]{1,0:T(4,128)S(1)} %get-tuple-element.66, ...), kind=kLoop, calls=%fused_computation.74 | loop fusion | flops 14667776 | bytes 8462336 | tf_op jit(solution)/shard_map/reduce_sum | solution.py:75
  404.2 3.8 multiply_reduce_fusion.29
  (150 shorter events, 42.0 us)
Async XLA Ops:
  7.2 289.1 %copy-start = (bf16[32,16,256]{2,1,0:T(8,128)(2,1)S(1)}, bf16[32,16,256]{2,1,0:T(8,128)(2,1)}, u32[]{:S(2)}) copy-start(bf16[32,16,256]{2,1,0:T(8,128)(2,1)} %param.7) | copy-start | bytes 786436
  7.2 287.5 %all-gather.2.cloned.1.call-start = ((), (), s32[]{:S(2)}) async-start(), calls=%async_computation.3 | async-start | bytes 17756160 | tf_op jit(solution)/shard_map/all_gather | solution.py:55
  9.3 12.7 %all-to-all-start.2 = ((s32[16,4,8]{2,1,0:T(4,128)}), s32[16,4,8]{2,1,0:T(4,128)S(1)}, u32[]{:S(2)}, u32[]{:S(2)}) async-start(s32[16,4,8]{2,1,0:T(4,128)} %bitcast.25), calls=%async_computation.2 | async-start | bytes 65536 | tf_op jit(solution)/shard_map/all_to_all | solution.py:88
  22.0 14.8 %all-to-all-start = ((s32[16,4,8]{2,1,0:T(4,128)}), s32[16,4,8]{2,1,0:T(4,128)S(1)}, u32[]{:S(2)}, u32[]{:S(2)}) async-start(s32[16,4,8]{2,1,0:T(4,128)} %bitcast.22), calls=%async_computation | async-start | bytes 65536 | tf_op jit(solution)/shard_map/all_to_all | solution.py:89
  36.8 6.1 %copy-start.1 = (s32[2,64,2]{1,2,0:T(2,128)S(1)}, s32[2,64,2]{1,2,0:T(2,128)}, u32[]{:S(2)}) copy-start(s32[2,64,2]{1,2,0:T(2,128)} %param.11) | copy-start | bytes 3076
  36.8 137.5 %copy-start.2 = (bf16[2,128]{1,0:T(2,128)(2,1)S(1)}, bf16[2,128]{1,0:T(2,128)(2,1)}, u32[]{:S(2)}) copy-start(bf16[2,128]{1,0:T(2,128)(2,1)} %param.9) | copy-start | bytes 1540
  36.8 137.5 %all-to-all-start.1 = ((bf16[16,4,8,64,128]{4,3,2,1,0:T(8,128)(2,1)}), bf16[16,4,8,64,128]{4,3,2,1,0:T(8,128)(2,1)}, u32[]{:S(2)}, u32[]{:S(2)}) async-start(bf16[16,4,8,64,128]{4,3,2,1,0:T(8,128)(2,1)} %bitcast.260), calls=%async_computation.1 | async-start | bytes 16777216 | tf_op jit(solution)/shard_map/all_to_all | solution.py:87
Sparse Core Ops, SparseCore 0:
  10.7 283.9 all-gather.1
where the time goes:
time: 426 us; the launch traced here: 420 us
  waiting for transfers between devices  249 us (58%)
  other arithmetic  58.7 us (14%)
  matrix products  49.1 us (12%)
  local copies, waits for them, and re-layouts  31.7 us (7%)
  starting transfers between devices  16.4 us (4%)
  between operations  15 us (4%)
    all_to_all x1, waiting for transfers between devices, body(): lax.all_to_all(picked, 'frames', split_axis=0, concat_axis=0, tiled=True)  130 us
    all_gather x1, waiting for transfers between devices, body(): shard_piece = lax.all_gather(coarse_feat, 'blk', axis=1, tiled=True)  114 us
    reduce_sum x9, other arithmetic, body(): jnp.sum(weights * pos_row[None, None, :], axis=2)  55.3 us
    dot_general x16, matrix products, body(): jnp.einsum('rc,fpc->frp', query_rows, feat_block, preferred_element_type=...  43.3 us
    slice x2, local copies, waits for them, and re-layouts, body(): feat_block = shard_piece[:, offset:offset + 512]  11.9 us
    gather x1, local copies, waits for them, and re-layouts, body(): fine_tiles[jnp.arange(frames_here, dtype=jnp.int32)[None, :, None], list_...  10.3 us
  transfers between devices with their start and end apart: 4, of which 3 were waited for; matrix products, arithmetic and copies ran while one was open for 5% of the time, Pallas kernels for 0%

commit v1 on v0

--- a/solution.py
+++ b/solution.py
@@ -52,7 +52,9 @@
     query_rows = coarse_query.reshape(track_group * heads, channels)
     row_count = query_rows.shape[0]
     zeros_state = jnp.zeros((frames_here, row_count), jnp.float32)
-    shard_piece = lax.all_gather(coarse_feat, "blk", axis=1, tiled=True)
+    shard_piece = jnp.concatenate(
+        lax.all_to_all(jnp.stack([coarse_feat] * lax.axis_size("blk")), "blk", 0, 0), axis=1
+    )
     first_pos = jnp.int32(0)
     maxima = jnp.full((frames_here, row_count), -jnp.inf, jnp.float32)
     totals = zeros_state

time: 426 us -> 651 us (1.53)
  the two profiles are of different devices: /device:TPU:1 before, /device:TPU:131 now
where the time goes in v1:
time: 651 us; the launch traced here: 645 us
  waiting for transfers between devices  378 us (58%)
  blocking collectives  98.7 us (15%)
  other arithmetic  58.7 us (9%)
  matrix products  49.1 us (8%)
  local copies, waits for them, and re-layouts  39 us (6%)
  starting transfers between devices  20.1 us (3%)
    all_to_all x1, waiting for transfers between devices, body(): lax.all_to_all(jnp.stack([coarse_feat] * lax.axis_size('blk')), 'blk', 0, 0)  374 us
    all_to_all x1, blocking collectives, body(): lax.all_to_all(picked, 'frames', split_axis=0, concat_axis=0, tiled=True)  98.7 us
    reduce_sum x9, other arithmetic, body(): jnp.sum(weights * pos_row[None, None, :], axis=2)  55.3 us
    dot_general x16, matrix products, body(): jnp.einsum('rc,fpc->frp', query_rows, feat_block, preferred_element_type=...  43.3 us
  transfers between devices with their start and end apart: 3, of which 2 were waited for; matrix products, arithmetic and copies ran while one was open for 3% of the time, Pallas kernels for 0%

profile of v1, /device:TPU:131, one launch (start us, length us, event | category | flops | bytes accessed | tf_op | source)
XLA Modules:
  0.0 644.8 jit_solution(7219744034755076218)
XLA Ops:
  2.1 6.2 all-to-all-start.3
  9.6 3.3 all-to-all-done.3
  13.0 4.8 all-to-all-start.1
  18.6 9.8 %gather_fusion = bf16[512,64,128]{2,1,0:T(8,128)(2,1)} fusion(bf16[4,64,64,128]{3,2,1,0:T(8,128)(2,1)} %param.10, s32[512]{0:T(512)S(1)} %reshape.900), kind=kCustom, calls=%fused_computation | custom fusion | bytes 16781312 | tf_op jit(solution)/shard_map/gather | solution.py:86
  28.5 98.7 %all_to_all.20 = bf16[16,4,8,64,128]{4,3,2,1,0:T(8,128)(2,1)} all-to-all(bf16[16,4,8,64,128]{4,3,2,1,0:T(8,128)(2,1)} %bitcast.263), channel_id=1, replica_groups=mesh['blk'=16,'frames'=16] {'frames'}, dimensions={0} | all-to-all | bytes 16777216 | tf_op jit(solution)/shard_map/all_to_all | solution.py:89
  127.2 7.7 %stack.6 = bf16[16,4,510,256]{3,1,2,0:T(4,128)(2,1)} broadcast(bf16[4,510,256]{2,0,1:T(4,128)(2,1)S(1)} %copy-done.1), dimensions={1,2,3} | broadcast | bytes 17756160 | tf_op jit(solution)/shard_map/stack | solution.py:56
  134.9 9.1 %all-to-all-start = ((bf16[16,4,510,256]{3,1,2,0:T(4,128)(2,1)}), bf16[16,4,510,256]{3,1,2,0:T(4,128)(2,1)}, u32[]{:S(2)}, u32[]{:S(2)}) async-start(bf16[16,4,510,256]{3,1,2,0:T(4,128)(2,1)} %stack.6), calls=%async_computation | async-start | bytes 33423360 | tf_op jit(solution)/shard_map/all_to_all | solution.py:56
  145.8 5.8 multiply_reduce_fusion.33
  152.4 374.2 %all-to-all-done = bf16[16,4,510,256]{3,1,2,0:T(4,128)(2,1)} async-done(((bf16[16,4,510,256]{3,1,2,0:T(4,128)(2,1)}), bf16[16,4,510,256]{3,1,2,0:T(4,128)(2,1)}, u32[]{:S(2)}, u32[]{:S(2)}) %all-to-all-start) | async-done | bytes 16711712 | tf_op jit(solution)/shard_map/all_to_all | solution.py:56
  528.2 10.4 %fusion.197 = (bf16[4,512,256]{2,0,1:T(4,128)(2,1)S(1)}, bf16[4,512,256]{2,0,1:T(4,128)(2,1)S(1)}, bf16[4,512,256]{2,0,1:T(4,128)(2,1)S(1)}, bf16[4,512,256]{2,0...) fusion(bf16[4,8160,256]{2,0,1:T(4,128)(2,1)} %bitcast.1), kind=kLoop, calls=%fused_computation.377 | loop fusion | bytes 31457280 | tf_op jit(solution)/shard_map/slice | solution.py:65
  541.2 2.7 bitcast_reduce_fusion
  543.9 2.7 bitcast_reduce_fusion.1
  554.7 2.7 bitcast_reduce_fusion.5
  560.2 2.8 bitcast_reduce_fusion.7
  571.0 2.8 bitcast_reduce_fusion.11
  583.4 3.8 multiply_reduce_fusion.31
  587.3 6.8 %multiply_reduce_fusion.15 = (f32[4,512]{1,0:T(4,128)S(1)}, f32[4,512]{1,0:T(4,128)S(1)}, f32[4,512]{1,0:T(4,128)S(1)}, f32[4,512]{1,0:T(4,128)S(1)}, f32[4,512]{1,0:T(4,128)S(1)}, /*index=5*/f32[4,512]{1,0:T(4,128)S(1)}) fusion(f32[4,512,512]{2,1,0:T(8,128)} %get-tuple-element.96, f32[512]{0:T(512)S(1)} %fusion.108, f32[4,512]{1,0:T(4,128)S(1)} %get-tuple-element.54, ...), kind=kLoop, calls=%fused_computation.62 | loop fusion | flops 14667776 | bytes 8462336 | tf_op jit(solution)/shard_map/reduce_sum | solution.py:77
  594.2 6.8 %multiply_reduce_fusion.17 = (f32[4,512]{1,0:T(4,128)S(1)}, f32[4,512]{1,0:T(4,128)S(1)}, f32[4,512]{1,0:T(4,128)S(1)}, f32[4,512]{1,0:T(4,128)S(1)}, f32[4,512]{1,0:T(4,128)S(1)}, /*index=5*/f32[4,512]{1,0:T(4,128)S(1)}) fusion(f32[4,512,512]{2,1,0:T(8,128)} %get-tuple-element.100, f32[512]{0:T(512)S(1)} %fusion.116, f32[4,512]{1,0:T(4,128)S(1)} %get-tuple-element.56, ...), kind=kLoop, calls=%fused_computation.64 | loop fusion | flops 14667776 | bytes 8462336 | tf_op jit(solution)/shard_map/reduce_sum | solution.py:77
  601.2 6.8 %multiply_reduce_fusion.19 = (f32[4,512]{1,0:T(4,128)S(1)}, f32[4,512]{1,0:T(4,128)S(1)}, f32[4,512]{1,0:T(4,128)S(1)}, f32[4,512]{1,0:T(4,128)S(1)}, f32[4,512]{1,0:T(4,128)S(1)}, /*index=5*/f32[4,512]{1,0:T(4,128)S(1)}) fusion(f32[4,512,512]{2,1,0:T(8,128)} %get-tuple-element.104, f32[512]{0:T(512)S(1)} %fusion.124, f32[4,512]{1,0:T(4,128)S(1)} %get-tuple-element.58, ...), kind=kLoop, calls=%fused_computation.66 | loop fusion | flops 14667776 | bytes 8462336 | tf_op jit(solution)/shard_map/reduce_sum | solution.py:77
  608.2 6.8 %multiply_reduce_fusion.21 = (f32[4,512]{1,0:T(4,128)S(1)}, f32[4,512]{1,0:T(4,128)S(1)}, f32[4,512]{1,0:T(4,128)S(1)}, f32[4,512]{1,0:T(4,128)S(1)}, f32[4,512]{1,0:T(4,128)S(1)}, /*index=5*/f32[4,512]{1,0:T(4,128)S(1)}) fusion(f32[4,512,512]{2,1,0:T(8,128)} %get-tuple-element.108, f32[512]{0:T(512)S(1)} %fusion.132, f32[4,512]{1,0:T(4,128)S(1)} %get-tuple-element.60, ...), kind=kLoop, calls=%fused_computation.68 | loop fusion | flops 14667776 | bytes 8462336 | tf_op jit(solution)/shard_map/reduce_sum | solution.py:77
  615.1 7.0 %multiply_reduce_fusion.23 = (f32[4,512]{1,0:T(4,128)S(1)}, f32[4,512]{1,0:T(4,128)S(1)}, f32[4,512]{1,0:T(4,128)S(1)}, f32[4,512]{1,0:T(4,128)S(1)}, f32[4,512]{1,0:T(4,128)S(1)}, /*index=5*/f32[4,512]{1,0:T(4,128)S(1)}) fusion(f32[4,512,512]{2,1,0:T(8,128)} %get-tuple-element.112, f32[512]{0:T(512)S(1)} %fusion.140, f32[4,512]{1,0:T(4,128)S(1)} %get-tuple-element.62, ...), kind=kLoop, calls=%fused_computation.70 | loop fusion | flops 14667776 | bytes 8462336 | tf_op jit(solution)/shard_map/reduce_sum | solution.py:77
  622.3 6.8 %multiply_reduce_fusion.25 = (f32[4,512]{1,0:T(4,128)S(1)}, f32[4,512]{1,0:T(4,128)S(1)}, f32[4,512]{1,0:T(4,128)S(1)}, f32[4,512]{1,0:T(4,128)S(1)}, f32[4,512]{1,0:T(4,128)S(1)}, /*index=5*/f32[4,512]{1,0:T(4,128)S(1)}) fusion(f32[4,512,512]{2,1,0:T(8,128)} %get-tuple-element.116, f32[512]{0:T(512)S(1)} %fusion.148, f32[4,512]{1,0:T(4,128)S(1)} %get-tuple-element.64, ...), kind=kLoop, calls=%fused_computation.72 | loop fusion | flops 14667776 | bytes 8462336 | tf_op jit(solution)/shard_map/reduce_sum | solution.py:77
  629.3 6.8 %multiply_reduce_fusion.27 = (f32[4,512]{1,0:T(4,128)S(1)}, f32[4,512]{1,0:T(4,128)S(1)}, f32[4,512]{1,0:T(4,128)S(1)}, f32[4,512]{1,0:T(4,128)S(1)}, f32[4,512]{1,0:T(4,128)S(1)}, /*index=5*/f32[4,512]{1,0:T(4,128)S(1)}) fusion(f32[4,512,512]{2,1,0:T(8,128)} %get-tuple-element.120, f32[512]{0:T(512)S(1)} %fusion.156, f32[4,512]{1,0:T(4,128)S(1)} %get-tuple-element.66, ...), kind=kLoop, calls=%fused_computation.74 | loop fusion | flops 14667776 | bytes 8462336 | tf_op jit(solution)/shard_map/reduce_sum | solution.py:77
  636.2 3.8 multiply_reduce_fusion.29
  (151 shorter events, 44.0 us)
Async XLA Ops:
  0.6 537.9 %copy-start = (bf16[32,16,256]{2,1,0:T(8,128)(2,1)S(1)}, bf16[32,16,256]{2,1,0:T(8,128)(2,1)}, u32[]{:S(2)}) copy-start(bf16[32,16,256]{2,1,0:T(8,128)(2,1)} %param.7) | copy-start | bytes 786436
  2.1 10.9 %all-to-all-start.3 = ((s32[16,4,8]{2,1,0:T(4,128)}), s32[16,4,8]{2,1,0:T(4,128)S(1)}, u32[]{:S(2)}, u32[]{:S(2)}) async-start(s32[16,4,8]{2,1,0:T(4,128)} %bitcast.28), calls=%async_computation.3 | async-start | bytes 65536 | tf_op jit(solution)/shard_map/all_to_all | solution.py:90
  13.0 15.5 %all-to-all-start.1 = ((s32[16,4,8]{2,1,0:T(4,128)}), s32[16,4,8]{2,1,0:T(4,128)S(1)}, u32[]{:S(2)}, u32[]{:S(2)}) async-start(s32[16,4,8]{2,1,0:T(4,128)} %bitcast.25), calls=%async_computation.1 | async-start | bytes 65536 | tf_op jit(solution)/shard_map/all_to_all | solution.py:91
  28.5 98.7 %copy-start.1 = (bf16[4,510,256]{2,0,1:T(4,128)(2,1)S(1)}, bf16[4,510,256]{2,0,1:T(4,128)(2,1)}, u32[]{:S(2)}) copy-start(bf16[4,510,256]{2,0,1:T(4,128)(2,1)} %param.8) | copy-start | bytes 3133444
  134.9 9.3 %copy-start.2 = (s32[2,64,2]{1,2,0:T(2,128)S(1)}, s32[2,64,2]{1,2,0:T(2,128)}, u32[]{:S(2)}) copy-start(s32[2,64,2]{1,2,0:T(2,128)} %param.11) | copy-start | bytes 3076
  134.9 10.9 %copy-start.3 = (bf16[2,128]{1,0:T(2,128)(2,1)S(1)}, bf16[2,128]{1,0:T(2,128)(2,1)}, u32[]{:S(2)}) copy-start(bf16[2,128]{1,0:T(2,128)(2,1)} %param.9) | copy-start | bytes 1540
  134.9 391.7 %all-to-all-start = ((bf16[16,4,510,256]{3,1,2,0:T(4,128)(2,1)}), bf16[16,4,510,256]{3,1,2,0:T(4,128)(2,1)}, u32[]{:S(2)}, u32[]{:S(2)}) async-start(bf16[16,4,510,256]{3,1,2,0:T(4,128)(2,1)} %stack.6), calls=%async_computation | async-start | bytes 33423360 | tf_op jit(solution)/shard_map/all_to_all | solution.py:56
